TPU v7x, 32 devices: a whole 2x2x4 slice. The times are simulated.
32 devices in a mesh: exp: 8 (over y, x, core), strip: 4 (over z).
Axes of the slice: x: 2, y: 2, z: 4, core: 2. Of those that a mesh axis runs over, the one named last changes fastest.
Arguments:
- science: float32 [8, 512, 2048], P('exp', 'strip'), may hold values from -30 to 30
- variance: float32 [8, 512, 2048], P('exp', 'strip'), may hold values from 0.25 to 4
- template: float32 [576, 2176], P(None, 'exp'), may hold values from -14 to 14
- offset_rows: int32 [8], P('exp'), may hold values from 0 to 24
- offset_cols: int32 [8], P('exp'), may hold values from 0 to 88
- stamp_rows: int32 [8, 64], P('exp', 'strip'), may hold values from 0 to 96
- stamp_cols: int32 [8, 64], P('exp', 'strip'), may hold values from 0 to 2016
Outputs:
- difference: float32 [8, 512, 2048], P('exp', 'strip')
All inputs are finite; a program needn't handle non-finite values.
Results may differ from a plain program's by a relative error of at most 0.0047.
Values sent between devices are 32-bit elements; how exact they have to be, the bound alone decides.
A program may use at most 128 MiB of HBM per device.

v0:
```python
import functools

import jax
import jax.numpy as jnp
import ml_dtypes
import numpy as np
from jax import lax
from jax.experimental import pallas as pl
from jax.experimental.pallas import tpu as pltpu
from jax.sharding import PartitionSpec as P

STAMP_SIZE = 32
STAMP_COUNT = 16
BASES = 27
SPATIAL_TERMS = 6
BACKGROUND_TERMS = 3
KERNEL_HALF = 20
TAPS = 2 * KERNEL_HALF + 1
UNKNOWNS = 165
SHIFT_MAX_ROWS = 24

SIGMAS = (1.0, 2.0, 4.0)
DEGREES = (4, 2, 2)
RIDGE = 0.001

SLOT = 32
SYSTEM = SLOT * SPATIAL_TERMS
FILTERS = 11
PACKED = SYSTEM + SYSTEM - 128
GROUP = 4
MODEL_TILES = 4
MESH = pl.DeviceIdType.MESH
BF16 = ml_dtypes.bfloat16


def filter_table():
    offsets = np.arange(-KERNEL_HALF, KERNEL_HALF + 1).astype(np.float64)
    entries = []
    for spread, degree in zip(SIGMAS, DEGREES):
        profile = np.exp(-offsets * offsets / (2.0 * spread * spread))
        profile = profile / np.sum(profile)
        for exponent in range(degree + 1):
            entries.append((offsets / spread) ** exponent * profile)
    return np.stack(entries).astype(np.float32)


def filter_groups():
    groups = []
    first_filter = 0
    basis = 0
    for gaussian, degree in enumerate(DEGREES):
        members = [[] for _ in range(degree + 1)]
        for across in range(degree + 1):
            for down in range(degree + 1 - across):
                members[down].append((basis, across))
                basis += 1
        for down in range(degree + 1):
            groups.append((first_filter + down, gaussian, members[down]))
        first_filter += degree + 1
    return groups


def split_band(table, out_rows, in_rows, depth):
    band = np.zeros((table.shape[0], out_rows, in_rows), np.float32)
    for r in range(out_rows):
        band[:, r, r : r + TAPS] = table
    high = band.astype(BF16)
    low = (band - high.astype(np.float32)).astype(BF16)
    full = np.zeros((table.shape[0], out_rows, depth), BF16)
    full[:, :, 0:in_rows] = high
    full[:, :, in_rows : 2 * in_rows] = high
    full[:, :, 2 * in_rows : 3 * in_rows] = low
    return full.reshape(table.shape[0] * out_rows, depth)


def stamp_bands(table):
    result = []
    first = 0
    for degree in DEGREES:
        band = np.zeros((GROUP * 128, (degree + 1) * 128), np.float32)
        for a in range(degree + 1):
            for s in range(GROUP):
                for c in range(STAMP_SIZE):
                    band[s * 128 + c : s * 128 + c + TAPS, a * 128 + s * 32 + c] = table[first + a]
        result.append(band.astype(BF16))
        first += degree + 1
    return result


def across_bands(table):
    result = []
    first = 0
    for degree in DEGREES:
        band = np.zeros((256, (degree + 1) * 128), np.float32)
        for a in range(degree + 1):
            for c in range(128):
                band[c : c + TAPS, a * 128 + c] = table[first + a]
        result.append(band.astype(BF16))
        first += degree + 1
    return result


def split(value):
    high = value.astype(jnp.bfloat16)
    low = (value - high.astype(jnp.float32)).astype(jnp.bfloat16)
    return high, low


def cut(source, top, tile, height):
    read = height + 8
    first = jnp.minimum(top // 8, (source.shape[0] - read) // 8) * 8
    block = source[
        pl.ds(pl.multiple_of(first, 8), read), pl.ds(pl.multiple_of(tile * 128, 128), 256)
    ]
    return pltpu.roll(block, lax.rem(read - (top - first), read), 0)[:height]


def stamp_kernel(
    image_rows, columns, place, rows, cols, win, sci, var, vband, h0, h1, h2,
    out, patch, vert, basis, weight, design,
):
    shift_down, shift_side, row_base = place[0], place[1], place[2]
    win_tiles = win.shape[1] // 128
    sci_tiles = columns // 128
    bands = (h0, h1, h2)
    pad = jnp.zeros((8, 128), jnp.float32)
    lane = lax.broadcasted_iota(jnp.int32, (STAMP_SIZE, 128), 1)
    for g in range(STAMP_COUNT // GROUP):
        sci_group = jnp.zeros((STAMP_SIZE, 128), jnp.float32)
        var_group = jnp.ones((STAMP_SIZE, 128), jnp.float32)
        for i in range(GROUP):
            s = g * GROUP + i
            top, left = rows[s], cols[s]
            start = shift_side + left
            tile = jnp.minimum(start // 128, win_tiles - 2)
            shift = start - tile * 128
            piece = cut(win, shift_down + top, tile, 72)
            piece = pltpu.roll(piece, lax.rem(256 - shift, 256), 1)[:, :128]
            piece = jnp.concatenate([piece, pad], 0)
            high, low = split(piece)
            patch[:, i * 128 : (i + 1) * 128] = jnp.concatenate(
                [high, low, high, jnp.zeros((16, 128), jnp.bfloat16)], 0
            )
            tile = jnp.minimum(left // 128, sci_tiles - 2)
            shift = lax.rem(256 + i * STAMP_SIZE - (left - tile * 128), 256)
            inside = (lane >= i * STAMP_SIZE) & (lane < (i + 1) * STAMP_SIZE)
            sci_group = jnp.where(inside, pltpu.roll(cut(sci, top, tile, STAMP_SIZE), shift, 1)[:, :128], sci_group)
            var_group = jnp.where(inside, pltpu.roll(cut(var, top, tile, STAMP_SIZE), shift, 1)[:, :128], var_group)
        span = slice(g * STAMP_SIZE, (g + 1) * STAMP_SIZE)
        weight[span, :] = 1.0 / jnp.sqrt(var_group)
        basis[28 * 128 + g * STAMP_SIZE : 28 * 128 + (g + 1) * STAMP_SIZE, :] = sci_group
        filtered = jnp.dot(vband[...], patch[...], preferred_element_type=jnp.float32)
        for m in range(FILTERS):
            vert[m * 128 + g * 32 : m * 128 + g * 32 + 32, :] = filtered[
                m * 32 : m * 32 + 32
            ].astype(jnp.bfloat16)
    basis[27 * 128 : 28 * 128, :] = jnp.ones((128, 128), jnp.float32)
    basis[29 * 128 :, :] = jnp.zeros((3 * 128, 128), jnp.float32)
    for m, gaussian, members in filter_groups():
        width = len(members) * 128
        result = jnp.dot(
            vert[m * 128 : (m + 1) * 128, :],
            bands[gaussian][:, :width],
            preferred_element_type=jnp.float32,
        )
        for k, a in members:
            basis[k * 128 : (k + 1) * 128, :] = result[:, a * 128 : (a + 1) * 128]

    lane_row = lax.broadcasted_iota(jnp.int32, (1, 128), 1)
    total = jnp.zeros((SYSTEM, SYSTEM), jnp.float32)
    contract = (((1,), (1,)), ((), ()))
    for g in range(STAMP_COUNT // GROUP):
        tops = jnp.zeros((1, 128), jnp.int32)
        lefts = jnp.zeros((1, 128), jnp.int32)
        for i in range(GROUP):
            inside = (lane_row >= i * STAMP_SIZE) & (lane_row < (i + 1) * STAMP_SIZE)
            tops = jnp.where(inside, rows[g * GROUP + i], tops)
            lefts = jnp.where(inside, cols[g * GROUP + i] - i * STAMP_SIZE, lefts)
        x = (2.0 * (lefts + lane_row).astype(jnp.float32) + 1.0 - columns) / columns
        tops = tops + row_base

        def one_row(r, carry):
            at = g * STAMP_SIZE + r
            y = (2.0 * (tops + r).astype(jnp.float32) + 1.0 - image_rows) / image_rows
            images = basis[pl.ds(at, SLOT, stride=128), :]
            images = images * weight[pl.ds(at, 1), :]
            place_at = pl.ds(pl.multiple_of(r * 128, 128), 128)
            for j, term in enumerate((None, x, y, x * x, x * y, y * y)):
                value = images if term is None else images * term
                design[j * SLOT : (j + 1) * SLOT, place_at] = value.astype(jnp.bfloat16)
            return carry

        lax.fori_loop(0, STAMP_SIZE, one_row, 0, unroll=4)
        total += lax.dot_general(
            design[...], design[...], contract, preferred_element_type=jnp.float32
        )
    total = jnp.concatenate([total, jnp.zeros((SYSTEM, 256 - SYSTEM), jnp.float32)], 1)
    out[:SYSTEM, :] = total[:, :128]
    out[SYSTEM:, :] = total[128:, 128:]


def is_unknown(j, k):
    return k < BASES or (k == BASES and j < BACKGROUND_TERMS)


def solve_kernel(normal, out):
    sums = normal[...]
    first = sums[:SYSTEM]
    corner = jnp.concatenate([first[128:], jnp.zeros((SYSTEM - 128, 128), jnp.float32)], 0)
    other = jnp.concatenate([corner.T, sums[SYSTEM:]], 0)
    sums = jnp.concatenate([first, other], 1)
    row = lax.broadcasted_iota(jnp.int32, sums.shape, 0)
    col = lax.broadcasted_iota(jnp.int32, sums.shape, 1)
    slot = row % SLOT
    used = (slot < BASES) | ((slot == BASES) & (row < SLOT * BACKGROUND_TERMS))
    system = jnp.where(used, sums, 0.0)
    diagonal = used & (row == col)
    trace = jnp.sum(jnp.where(diagonal, system, 0.0), axis=(0, 1), keepdims=True)
    system = system + jnp.where(diagonal, RIDGE * trace / UNKNOWNS, 0.0)
    local = lax.broadcasted_iota(jnp.int32, (SLOT // 8, 8, 256), 0) * 8
    local = local + lax.broadcasted_iota(jnp.int32, (SLOT // 8, 8, 256), 1)

    def twice(value):
        return jnp.concatenate([value, value], -1)

    def column(panel, at):
        return jnp.broadcast_to(panel[:, :, at : at + 1], (SLOT // 8, 8, 128))

    def line(value, k):
        return jnp.broadcast_to(value[k // 8, k % 8 : k % 8 + 1], (8, value.shape[2]))

    panels = []
    for j in range(SPATIAL_TERMS):
        panel = system[:SLOT].reshape(SLOT // 8, 8, 256)
        count = sum(is_unknown(j, k) for k in range(SLOT))
        for k in range(0, count - 1, 2):
            at = j * SLOT + k
            col0, col1 = column(panel, at), column(panel, at + 1)
            row0, row1 = line(panel, k), line(panel, k + 1)
            a, b, c, d = line(col0, k), line(col1, k), line(col0, k + 1), line(col1, k + 1)
            scale = 1.0 / (a * d - b * c)
            new0 = twice(d * scale) * row0 - twice(b * scale) * row1
            new1 = twice(a * scale) * row1 - twice(c * scale) * row0
            panel = panel - twice(col0) * new0[None] - twice(col1) * new1[None]
            panel = jnp.where(local == k, new0[None], jnp.where(local == k + 1, new1[None], panel))
        if count % 2:
            k = count - 1
            col = column(panel, j * SLOT + k)
            new = line(panel, k) * twice(1.0 / line(col, k))
            panel = jnp.where(local == k, new[None], panel - twice(col) * new[None])
        panel = panel.reshape(SLOT, 256)
        panels.append(panel)
        if j < SPATIAL_TERMS - 1:
            below = system[SLOT:]
            system = below - jnp.dot(
                below[:, j * SLOT : (j + 1) * SLOT],
                panel,
                precision=lax.Precision.HIGHEST,
                preferred_element_type=jnp.float32,
            )
    solved = [None] * SPATIAL_TERMS
    for j in reversed(range(SPATIAL_TERMS)):
        value = panels[j][:, :128]
        if j < SPATIAL_TERMS - 1:
            value = value - jnp.dot(
                panels[j][:, (j + 1) * SLOT : SYSTEM],
                jnp.concatenate(solved[j + 1 :], 0),
                precision=lax.Precision.HIGHEST,
                preferred_element_type=jnp.float32,
            )
        solved[j] = value
        out[j * SLOT : (j + 1) * SLOT, :] = jnp.broadcast_to(
            value[:, BASES + 1 : BASES + 2], (SLOT, 128)
        )


def gather_kernel(axis_size, own, out, send_sem, recv_sem, pass_sem, land_sem, own_sem):
    me = lax.axis_index("exp")
    sibling = me + 1 - 2 * lax.rem(me, 2)
    hops = axis_size // 2
    peers = [lax.rem(me + 2 * h, axis_size) for h in range(1, hops)]
    barrier = pltpu.get_barrier_semaphore()
    for peer in peers + [sibling]:
        pl.semaphore_signal(barrier, inc=1, device_id={"exp": peer}, device_id_type=MESH)
    pl.semaphore_wait(barrier, hops)
    copies = []
    for h, peer in enumerate(peers + [sibling]):
        copies.append(
            pltpu.make_async_remote_copy(
                src_ref=own,
                dst_ref=out.at[me],
                send_sem=send_sem.at[h],
                recv_sem=recv_sem.at[h],
                device_id={"exp": peer},
                device_id_type=MESH,
            )
        )
        copies[-1].start()
    keep = pltpu.make_async_copy(own, out.at[me], own_sem)
    keep.start()
    passed = []
    for h in range(hops - 1):
        copies[h].wait_recv()
        source = lax.rem(me - 2 * (h + 1) + axis_size, axis_size)
        passed.append(
            pltpu.make_async_remote_copy(
                src_ref=out.at[source],
                dst_ref=out.at[source],
                send_sem=pass_sem.at[h],
                recv_sem=land_sem.at[h],
                device_id={"exp": sibling},
                device_id_type=MESH,
            )
        )
        passed[-1].start()
    copies[-1].wait_recv()
    for copy in passed:
        copy.wait_recv()
    keep.wait()
    for copy in copies + passed:
        copy.wait_send()


def vertical_kernel(
    size, sums, window_hbm, band_hbm, total, out_hbm, landed, gathered, window, band, out,
    send_sem, recv_sem, give_sem, take_sem, in_sem, out_sem,
):
    me = lax.axis_index("strip")
    share = sums.shape[0] // size
    peers = [lax.rem(me + d, size) for d in range(1, size)]
    tiles = out.shape[1] // 256

    def one_tile(i, carry):
        at = pl.ds(pl.multiple_of(i * 256, 256), 256)
        out[:, at] = jnp.dot(
            band[...], window[:, at], preferred_element_type=jnp.float32
        ).astype(jnp.bfloat16)
        pltpu.make_async_copy(out.at[:, at], out_hbm.at[:, at], out_sem.at[i]).start()
        return carry

    def one_wait(i, carry):
        at = pl.ds(pl.multiple_of(i * 256, 256), 256)
        pltpu.make_async_copy(out.at[:, at], out_hbm.at[:, at], out_sem.at[i]).wait()
        return carry

    loads = [
        pltpu.make_async_copy(window_hbm, window, in_sem.at[0]),
        pltpu.make_async_copy(band_hbm, band, in_sem.at[1]),
    ]
    for load in loads:
        load.start()
    barrier = pltpu.get_barrier_semaphore()
    for peer in peers:
        pl.semaphore_signal(barrier, inc=1, device_id={"strip": peer}, device_id_type=MESH)
    pl.semaphore_wait(barrier, size - 1)
    scattered = []
    for d, peer in enumerate(peers):
        scattered.append(
            pltpu.make_async_remote_copy(
                src_ref=sums.at[pl.ds(pl.multiple_of(peer * share, 8), share), :],
                dst_ref=landed.at[d],
                send_sem=send_sem.at[d],
                recv_sem=recv_sem.at[d],
                device_id={"strip": peer},
                device_id_type=MESH,
            )
        )
        scattered[-1].start()
    for load in loads:
        load.wait()
    lax.fori_loop(0, tiles // 2, one_tile, 0)
    for copy in scattered:
        copy.wait_recv()
    mine = pl.ds(pl.multiple_of(me * share, 8), share)
    value = sums[mine, :]
    for d in range(size - 1):
        value = value + landed[d]
    gathered[mine, :] = value
    given = []
    for d, peer in enumerate(peers):
        given.append(
            pltpu.make_async_remote_copy(
                src_ref=gathered.at[mine, :],
                dst_ref=gathered.at[mine, :],
                send_sem=give_sem.at[d],
                recv_sem=take_sem.at[d],
                device_id={"strip": peer},
                device_id_type=MESH,
            )
        )
        given[-1].start()
    lax.fori_loop(tiles // 2, tiles, one_tile, 0)
    for copy in given:
        copy.wait_recv()
    total[...] = gathered[...]
    for copy in scattered + given:
        copy.wait_send()
    lax.fori_loop(0, tiles, one_wait, 0)


def model_kernel(image_rows, columns, place, solved, sci, left, right, h0, h1, h2, out, ya, yb):
    bands = (h0, h1, h2)
    step = pl.program_id(0)
    height = sci.shape[0]
    rows = lax.broadcasted_iota(jnp.int32, (height, 128), 0) + place[2]
    y = (2.0 * rows.astype(jnp.float32) + 1.0 - image_rows) / image_rows

    def coef(j, k):
        return solved[j * SLOT + k : j * SLOT + k + 1, :]

    @pl.when(step == 0)
    def _():
        for k in range(BASES):
            ya[k] = coef(0, k) + y * (coef(2, k) + y * coef(5, k))
            yb[k] = coef(1, k) + y * coef(4, k)

    xs = []
    for t in range(MODEL_TILES):
        cols = lax.broadcasted_iota(jnp.int32, (1, 128), 1) + (step * MODEL_TILES + t) * 128
        x = (2.0 * cols.astype(jnp.float32) + 1.0 - columns) / columns
        xs.append(x)
        at = slice(t * 128, (t + 1) * 128)
        out[:, at] = sci[:, at] - (
            coef(0, BASES) + coef(1, BASES) * x + coef(2, BASES) * y
        )
    for m, gaussian, members in filter_groups():
        at = slice(m * height, (m + 1) * height)
        row = jnp.concatenate([left[at, :], right[at, :]], 1)
        picture = jnp.concatenate(
            [row[:, t * 128 : t * 128 + 256] for t in range(MODEL_TILES)], 0
        )
        result = jnp.dot(
            picture, bands[gaussian][:, : len(members) * 128], preferred_element_type=jnp.float32
        )
        for t in range(MODEL_TILES):
            x = xs[t]
            part = result[t * height : (t + 1) * height]
            value = out[:, t * 128 : (t + 1) * 128]
            for k, a in members:
                field = ya[k] + x * (yb[k] + x * coef(3, k))
                value = value - field * part[:, a * 128 : (a + 1) * 128]
            out[:, t * 128 : (t + 1) * 128] = value


def shards(science, variance, template, offset_rows, offset_cols, stamp_rows, stamp_cols):
    strip_rows = science.shape[1]
    columns = science.shape[2]
    strip_count = lax.axis_size("strip")
    strip_index = lax.axis_index("strip")
    image_rows = strip_rows * strip_count
    window_rows = strip_rows + 2 * KERNEL_HALF
    table = filter_table()
    short = table.astype(BF16).astype(np.float32)
    row_base = strip_index * strip_rows
    exposures = lax.axis_size("exp")
    own_cols = template.shape[1]
    gather_rows = window_rows + SHIFT_MAX_ROWS
    anywhere = pl.BlockSpec(memory_space=pl.ANY)
    blocks = pl.pallas_call(
        functools.partial(gather_kernel, exposures),
        out_shape=jax.ShapeDtypeStruct((exposures, own_cols, gather_rows), jnp.float32),
        in_specs=[anywhere],
        out_specs=anywhere,
        scratch_shapes=[
            pltpu.SemaphoreType.DMA((exposures // 2,)),
            pltpu.SemaphoreType.DMA((exposures // 2,)),
            pltpu.SemaphoreType.DMA((max(exposures // 2 - 1, 1),)),
            pltpu.SemaphoreType.DMA((max(exposures // 2 - 1, 1),)),
            pltpu.SemaphoreType.DMA,
        ],
        compiler_params=pltpu.CompilerParams(collective_id=0, has_side_effects=True),
        name="gather",
    )(lax.dynamic_slice_in_dim(template, row_base, gather_rows, 0).T)
    strip = blocks.reshape(exposures * own_cols, gather_rows).T
    place = jnp.stack([offset_rows[0], offset_cols[0], row_base.astype(jnp.int32)])
    science = science[0]
    variance = variance[0]
    smem = pl.BlockSpec(memory_space=pltpu.SMEM)
    vmem = pl.BlockSpec(memory_space=pltpu.VMEM)
    limit = pltpu.CompilerParams(vmem_limit_bytes=56 * 1024 * 1024)
    across = [jnp.asarray(b) for b in across_bands(short)]

    normal = pl.pallas_call(
        functools.partial(stamp_kernel, image_rows, columns),
        out_shape=jax.ShapeDtypeStruct((PACKED, 128), jnp.float32),
        in_specs=[smem] * 3 + [vmem] * 7,
        out_specs=vmem,
        scratch_shapes=[
            pltpu.VMEM((256, GROUP * 128), jnp.bfloat16),
            pltpu.VMEM((FILTERS * 128, GROUP * 128), jnp.bfloat16),
            pltpu.VMEM((SLOT * 128, 128), jnp.float32),
            pltpu.VMEM((128, 128), jnp.float32),
            pltpu.VMEM((SYSTEM, STAMP_SIZE * 128), jnp.bfloat16),
        ],
        compiler_params=limit,
        name="stamp_sums",
    )(
        place,
        stamp_rows[0],
        stamp_cols[0],
        strip,
        science,
        variance,
        jnp.asarray(split_band(table, STAMP_SIZE, 80, 256)),
        *[jnp.asarray(b) for b in stamp_bands(short)],
    )
    wide = -(-(columns + 128) // 256) * 256
    window = lax.dynamic_slice(
        strip, (offset_rows[0], offset_cols[0]), (window_rows, columns + 2 * KERNEL_HALF)
    )
    window = jnp.pad(window, ((0, 0), (0, wide - window.shape[1])))
    high = lax.reduce_precision(window, 8, 7)
    low = window - high
    depth = -(-3 * window_rows // 256) * 256
    filler = jnp.zeros((depth - 3 * window_rows, wide), jnp.float32)
    share = PACKED // strip_count
    copies = (strip_count - 1,)
    normal, vertical = pl.pallas_call(
        functools.partial(vertical_kernel, strip_count),
        out_shape=(
            jax.ShapeDtypeStruct((PACKED, 128), jnp.float32),
            jax.ShapeDtypeStruct((FILTERS * strip_rows, wide), jnp.bfloat16),
        ),
        in_specs=[vmem, anywhere, anywhere],
        out_specs=(vmem, anywhere),
        scratch_shapes=[
            pltpu.VMEM((strip_count - 1, share, 128), jnp.float32),
            pltpu.VMEM((PACKED, 128), jnp.float32),
            pltpu.VMEM((depth, wide), jnp.bfloat16),
            pltpu.VMEM((FILTERS * strip_rows, depth), jnp.bfloat16),
            pltpu.VMEM((FILTERS * strip_rows, wide), jnp.bfloat16),
            pltpu.SemaphoreType.DMA(copies),
            pltpu.SemaphoreType.DMA(copies),
            pltpu.SemaphoreType.DMA(copies),
            pltpu.SemaphoreType.DMA(copies),
            pltpu.SemaphoreType.DMA((2,)),
            pltpu.SemaphoreType.DMA((wide // 256,)),
        ],
        compiler_params=pltpu.CompilerParams(
            vmem_limit_bytes=56 * 1024 * 1024, collective_id=1, has_side_effects=True
        ),
        name="vertical",
    )(
        normal,
        jnp.concatenate([high, low, high, filler], 0).astype(jnp.bfloat16),
        jnp.asarray(split_band(table, strip_rows, window_rows, depth)),
    )

    solved = pl.pallas_call(
        solve_kernel,
        out_shape=jax.ShapeDtypeStruct((SYSTEM, 128), jnp.float32),
        in_specs=[vmem],
        out_specs=vmem,
        compiler_params=limit,
        name="solve",
    )(normal)

    rows_all = FILTERS * strip_rows
    step_cols = 128 * MODEL_TILES
    difference = pl.pallas_call(
        functools.partial(model_kernel, image_rows, columns),
        grid=(columns // step_cols,),
        out_shape=jax.ShapeDtypeStruct((strip_rows, columns), jnp.float32),
        in_specs=[
            smem,
            pl.BlockSpec((SYSTEM, 128), lambda i: (0, 0)),
            pl.BlockSpec((strip_rows, step_cols), lambda i: (0, i)),
            pl.BlockSpec((rows_all, step_cols), lambda i: (0, i)),
            pl.BlockSpec((rows_all, 128), lambda i: (0, MODEL_TILES * (i + 1))),
        ]
        + [pl.BlockSpec(b.shape, lambda i: (0, 0)) for b in across],
        out_specs=pl.BlockSpec((strip_rows, step_cols), lambda i: (0, i)),
        scratch_shapes=[
            pltpu.VMEM((BASES, strip_rows, 128), jnp.float32),
            pltpu.VMEM((BASES, strip_rows, 128), jnp.float32),
        ],
        compiler_params=limit,
        name="model",
    )(place, solved, science, vertical, vertical, *across)
    return difference[None]


def solution(mesh):
    in_specs = (
        P("exp", "strip", None),
        P("exp", "strip", None),
        P(None, "exp"),
        P("exp"),
        P("exp"),
        P("exp", "strip"),
        P("exp", "strip"),
    )
    out_specs = P("exp", "strip", None)
    return jax.shard_map(shards, mesh=mesh, in_specs=in_specs, out_specs=out_specs, check_vma=False)
```

profile of v0, /device:TPU:0, one launch (start us, length us, event | category | flops | bytes accessed | tf_op | source)
XLA Modules:
  0.0 79.1 jit_solution(16714860972790268333)
XLA Ops:
  0.0 0.0 copy-start
  1.4 0.7 pad_add_fusion.place
  2.0 0.1 pad.8.clone
  2.1 0.0 copy-done
  2.1 0.9 %dynamic-slice_bitcast_fusion.1.own = f32[272,192]{1,0:T(8,128)} fusion(f32[576,272]{0,1:T(8,128)S(1)} %copy-done, s32[]{:T(128)S(6)} %select_n.9), kind=kLoop, calls=%fused_computation.5 | loop fusion | bytes 417796 | tf_op jit(solution)/shard_map/transpose | solution.py:473
  3.0 19.2 %gather.1 = f32[8,272,192]{2,1,0:T(8,128)} custom-call(f32[272,192]{1,0:T(8,128)} %dynamic-slice_bitcast_fusion.1.own), custom_call_target="tpu_custom_call" | custom-call | tf_op jit(solution)/shard_map/gather/pallas_call | solution.py:459
  22.2 2.9 %copy.18 = f32[2176,192]{0,1:T(8,128)} copy(f32[2176,192]{1,0:T(8,128)} %bitcast.21) | data formatting | bytes 3342336 | tf_op jit(solution)/shard_map/reshape | solution.py:474
  25.1 0.0 copy-start.1
  25.1 11.4 %stamp_sums.1.sums = f32[256,128]{1,0:T(8,128)} custom-call(s32[3]{0:T(128)} %pad_add_fusion.place, s32[16]{0:T(128)} %bitcast.25, s32[16]{0:T(128)} %bitcast.26, f32[192,2176]{1,0:T(8,128)} %bitcast.20, f32[128,2048]{1,0:T(8,128)} %bitcast.22, f32[128,2048]{1,0:T(8,128)} %bitcast.24, bf16[352,256]{1,0:T(8,128)(2,1)} %constant.38.clone.vband, ...), custom_call_target="tpu_custom_call" | custom-call | tf_op jit(solution)/shard_map/stamp_sums/pallas_call | solution.py:483
  36.5 0.0 copy-done.1
  36.5 0.4 dynamic-slice_bitcast_fusion
  37.0 0.2 fusion
  37.2 1.9 %maximum_maximum_fusion.window_hbm = bf16[512,2304]{1,0:T(8,128)(2,1)} fusion(bf16[168,2304]{1,0:T(8,128)(2,1)S(1)} %get-tuple-element.10, bf16[168,2304]{1,0:T(8,128)(2,1)S(1)} %get-tuple-element.9, bf16[512]{0:T(512)(128)(2,1)S(1)} %pad.8.clone), kind=kLoop, calls=%fused_computation | loop fusion | flops 9437184 | bytes 3908608 | tf_op jit(solution)/shard_map/concatenate | solution.py:545
  39.1 14.2 %vertical.1 = (f32[256,128]{1,0:T(8,128)}, bf16[1408,2304]{1,0:T(8,128)(2,1)}) custom-call(f32[256,128]{1,0:T(8,128)} %stamp_sums.1.sums, bf16[512,2304]{1,0:T(8,128)(2,1)} %maximum_maximum_fusion.window_hbm, bf16[1408,512]{1,0:T(8,128)(2,1)} %constant.42.clone.band_hbm), custom_call_target="tpu_custom_call" | custom-call | tf_op jit(solution)/shard_map/vertical/pallas_call | solution.py:518
  53.3 16.2 %solve.1.solved = f32[192,128]{1,0:T(8,128)} custom-call(f32[256,128]{1,0:T(8,128)} %get-tuple-element.7.normal), custom_call_target="tpu_custom_call" | custom-call | tf_op jit(solution)/shard_map/solve/pallas_call | solution.py:549
  69.4 9.6 %model.1 = f32[128,2048]{1,0:T(8,128)} custom-call(s32[3]{0:T(128)} %pad_add_fusion.place, f32[192,128]{1,0:T(8,128)} %solve.1.solved, f32[128,2048]{1,0:T(8,128)} %bitcast.23, bf16[1408,2304]{1,0:T(8,128)(2,1)} %get-tuple-element.8.left.right, bf16[1408,2304]{1,0:T(8,128)(2,1)} %get-tuple-element.8.left.right, bf16[256,640]{1,0:T(8,128)(2,1)} %constant.35.clone.h0, ...), custom_call_target="tpu_custom_call" | custom-call | tf_op jit(solution)/shard_map/model/pallas_call | solution.py:560
  (1 shorter events, 0.0 us)
Async XLA Ops:
  0.0 2.1 %copy-start = (f32[576,272]{0,1:T(8,128)S(1)}, f32[576,272]{0,1:T(8,128)}, u32[]{:S(2)}) copy-start(f32[576,272]{0,1:T(8,128)} %param.17) | copy-start | bytes 1880068
  25.1 11.4 %copy-start.1 = (f32[2176,192]{0,1:T(8,128)S(1)}, f32[2176,192]{0,1:T(8,128)}, u32[]{:S(2)}) copy-start(f32[2176,192]{0,1:T(8,128)} %copy.18) | copy-start | bytes 5013508
where the time goes:
time: 79.3 us; the launch traced here: 79.1 us
  Pallas kernels  70.6 us (89%)
  local copies, waits for them, and re-layouts  4.31 us (5%)
  other arithmetic  2.75 us (3%)
  between operations  1.41 us (2%)
    pallas_call x1, Pallas kernels, shards(): pl.pallas_call(functools.partial(gather_kernel, exposures), out_shape=jax...  19.2 us
    pallas_call x1, Pallas kernels, shards(): pl.pallas_call(solve_kernel, out_shape=jax.ShapeDtypeStruct((SYSTEM, 128)...  16.2 us
    pallas_call x1, Pallas kernels, shards(): pl.pallas_call(functools.partial(vertical_kernel, strip_count), out_shape...  14.2 us
    pallas_call x1, Pallas kernels, shards(): pl.pallas_call(functools.partial(stamp_kernel, image_rows, columns), out_...  11.4 us
    pallas_call x1, Pallas kernels, shards(): pl.pallas_call(functools.partial(model_kernel, image_rows, columns), grid...  9.62 us
    reshape x1, local copies, waits for them, and re-layouts, shards(): strip = blocks.reshape(exposures * own_cols, gather_rows).T  2.92 us
    concatenate x1, other arithmetic, shards(): jnp.concatenate([high, low, high, filler], 0).astype(jnp.bfloat16)  1.92 us

commit v1 on v0

--- a/solution.py
+++ b/solution.py
@@ -203,6 +203,39 @@
     return k < BASES or (k == BASES and j < BACKGROUND_TERMS)
 
 
+def invert_two(m):
+    (a, b), (c, d) = m
+    scale = 1.0 / (a * d - b * c)
+    return [[d * scale, -b * scale], [-c * scale, a * scale]]
+
+
+def times_two(p, q):
+    return [[p[i][0] * q[0][j] + p[i][1] * q[1][j] for j in range(2)] for i in range(2)]
+
+
+def less_two(p, q):
+    return [[p[i][j] - q[i][j] for j in range(2)] for i in range(2)]
+
+
+def invert_four(m):
+    p, q = [m[0][:2], m[1][:2]], [m[0][2:], m[1][2:]]
+    r, s = [m[2][:2], m[3][:2]], [m[2][2:], m[3][2:]]
+    p_inv = invert_two(p)
+    left = times_two(r, p_inv)
+    right = times_two(p_inv, q)
+    s_inv = invert_two(less_two(s, times_two(r, right)))
+    upper = times_two(right, s_inv)
+    lower = times_two(s_inv, left)
+    corner = times_two(upper, left)
+    top = [[p_inv[i][j] + corner[i][j] for j in range(2)] for i in range(2)]
+    return [
+        top[0] + [-v for v in upper[0]],
+        top[1] + [-v for v in upper[1]],
+        [-v for v in lower[0]] + s_inv[0],
+        [-v for v in lower[1]] + s_inv[1],
+    ]
+
+
 def solve_kernel(normal, out):
     sums = normal[...]
     first = sums[:SYSTEM]
@@ -233,7 +266,24 @@
     for j in range(SPATIAL_TERMS):
         panel = system[:SLOT].reshape(SLOT // 8, 8, 256)
         count = sum(is_unknown(j, k) for k in range(SLOT))
-        for k in range(0, count - 1, 2):
+        quads = count // 4 * 4
+        for k in range(0, quads, 4):
+            at = j * SLOT + k
+            cols = [column(panel, at + i) for i in range(4)]
+            rows = [line(panel, k + i) for i in range(4)]
+            entry = [[line(cols[m], k + i) for m in range(4)] for i in range(4)]
+            inverse = invert_four(entry)
+            news = []
+            for i in range(4):
+                new = twice(inverse[i][0]) * rows[0]
+                for m in range(1, 4):
+                    new = new + twice(inverse[i][m]) * rows[m]
+                news.append(new)
+            for i in range(4):
+                panel = panel - twice(cols[i]) * news[i][None]
+            for i in range(4):
+                panel = jnp.where(local == k + i, news[i][None], panel)
+        for k in range(quads, count - 1, 2):
             at = j * SLOT + k
             col0, col1 = column(panel, at), column(panel, at + 1)
             row0, row1 = line(panel, k), line(panel, k + 1)

time: 79.3 us -> 74.9 us (0.945)
  Pallas kernels: 70.6 us -> 66.2 us
    pallas_call x1, Pallas kernels: 16.2 us -> 11.8 us  [shards(): pl.pallas_call(solve_kernel, out_shape=jax.ShapeDtypeStruct((SYSTEM, 128)...]
where the time goes in v1:
time: 74.9 us; the launch traced here: 74.7 us
  Pallas kernels  66.2 us (88%)
  local copies, waits for them, and re-layouts  4.31 us (6%)
  other arithmetic  2.75 us (4%)
  between operations  1.41 us (2%)
    pallas_call x1, Pallas kernels, shards(): pl.pallas_call(functools.partial(gather_kernel, exposures), out_shape=jax...  19.2 us
    pallas_call x1, Pallas kernels, shards(): pl.pallas_call(functools.partial(vertical_kernel, strip_count), out_shape...  14.2 us
    pallas_call x1, Pallas kernels, shards(): pl.pallas_call(solve_kernel, out_shape=jax.ShapeDtypeStruct((SYSTEM, 128)...  11.8 us
    pallas_call x1, Pallas kernels, shards(): pl.pallas_call(functools.partial(stamp_kernel, image_rows, columns), out_...  11.4 us
    pallas_call x1, Pallas kernels, shards(): pl.pallas_call(functools.partial(model_kernel, image_rows, columns), grid...  9.63 us
    reshape x1, local copies, waits for them, and re-layouts, shards(): strip = blocks.reshape(exposures * own_cols, gather_rows).T  2.92 us
    concatenate x1, other arithmetic, shards(): jnp.concatenate([high, low, high, filler], 0).astype(jnp.bfloat16)  1.92 us

profile of v1, /device:TPU:0, one launch (start us, length us, event | category | flops | bytes accessed | tf_op | source)
XLA Modules:
  0.0 74.7 jit_solution(17526833027860145701)
XLA Ops:
  0.0 0.0 copy-start
  1.4 0.7 pad_add_fusion.place
  2.0 0.1 pad.8.clone
  2.1 0.0 copy-done
  2.1 0.9 %dynamic-slice_bitcast_fusion.1.own = f32[272,192]{1,0:T(8,128)} fusion(f32[576,272]{0,1:T(8,128)S(1)} %copy-done, s32[]{:T(128)S(6)} %select_n.9), kind=kLoop, calls=%fused_computation.5 | loop fusion | bytes 417796 | tf_op jit(solution)/shard_map/transpose | solution.py:523
  3.0 19.2 %gather.1 = f32[8,272,192]{2,1,0:T(8,128)} custom-call(f32[272,192]{1,0:T(8,128)} %dynamic-slice_bitcast_fusion.1.own), custom_call_target="tpu_custom_call" | custom-call | tf_op jit(solution)/shard_map/gather/pallas_call | solution.py:509
  22.2 2.9 %copy.18 = f32[2176,192]{0,1:T(8,128)} copy(f32[2176,192]{1,0:T(8,128)} %bitcast.21) | data formatting | bytes 3342336 | tf_op jit(solution)/shard_map/reshape | solution.py:524
  25.1 0.0 copy-start.1
  25.1 11.4 %stamp_sums.1.sums = f32[256,128]{1,0:T(8,128)} custom-call(s32[3]{0:T(128)} %pad_add_fusion.place, s32[16]{0:T(128)} %bitcast.25, s32[16]{0:T(128)} %bitcast.26, f32[192,2176]{1,0:T(8,128)} %bitcast.20, f32[128,2048]{1,0:T(8,128)} %bitcast.22, f32[128,2048]{1,0:T(8,128)} %bitcast.24, bf16[352,256]{1,0:T(8,128)(2,1)} %constant.38.clone.vband, ...), custom_call_target="tpu_custom_call" | custom-call | tf_op jit(solution)/shard_map/stamp_sums/pallas_call | solution.py:533
  36.5 0.0 copy-done.1
  36.5 0.4 dynamic-slice_bitcast_fusion
  37.0 0.2 fusion
  37.2 1.9 %maximum_maximum_fusion.window_hbm = bf16[512,2304]{1,0:T(8,128)(2,1)} fusion(bf16[168,2304]{1,0:T(8,128)(2,1)S(1)} %get-tuple-element.10, bf16[168,2304]{1,0:T(8,128)(2,1)S(1)} %get-tuple-element.9, bf16[512]{0:T(512)(128)(2,1)S(1)} %pad.8.clone), kind=kLoop, calls=%fused_computation | loop fusion | flops 9437184 | bytes 3908608 | tf_op jit(solution)/shard_map/concatenate | solution.py:595
  39.1 14.2 %vertical.1 = (f32[256,128]{1,0:T(8,128)}, bf16[1408,2304]{1,0:T(8,128)(2,1)}) custom-call(f32[256,128]{1,0:T(8,128)} %stamp_sums.1.sums, bf16[512,2304]{1,0:T(8,128)(2,1)} %maximum_maximum_fusion.window_hbm, bf16[1408,512]{1,0:T(8,128)(2,1)} %constant.42.clone.band_hbm), custom_call_target="tpu_custom_call" | custom-call | tf_op jit(solution)/shard_map/vertical/pallas_call | solution.py:568
  53.3 11.8 %solve.1.solved = f32[192,128]{1,0:T(8,128)} custom-call(f32[256,128]{1,0:T(8,128)} %get-tuple-element.7.normal), custom_call_target="tpu_custom_call" | custom-call | tf_op jit(solution)/shard_map/solve/pallas_call | solution.py:599
  65.1 9.6 %model.1 = f32[128,2048]{1,0:T(8,128)} custom-call(s32[3]{0:T(128)} %pad_add_fusion.place, f32[192,128]{1,0:T(8,128)} %solve.1.solved, f32[128,2048]{1,0:T(8,128)} %bitcast.23, bf16[1408,2304]{1,0:T(8,128)(2,1)} %get-tuple-element.8.left.right, bf16[1408,2304]{1,0:T(8,128)(2,1)} %get-tuple-element.8.left.right, bf16[256,640]{1,0:T(8,128)(2,1)} %constant.35.clone.h0, ...), custom_call_target="tpu_custom_call" | custom-call | tf_op jit(solution)/shard_map/model/pallas_call | solution.py:610
  (1 shorter events, 0.0 us)
Async XLA Ops:
  0.0 2.1 %copy-start = (f32[576,272]{0,1:T(8,128)S(1)}, f32[576,272]{0,1:T(8,128)}, u32[]{:S(2)}) copy-start(f32[576,272]{0,1:T(8,128)} %param.17) | copy-start | bytes 1880068
  25.1 11.4 %copy-start.1 = (f32[2176,192]{0,1:T(8,128)S(1)}, f32[2176,192]{0,1:T(8,128)}, u32[]{:S(2)}) copy-start(f32[2176,192]{0,1:T(8,128)} %copy.18) | copy-start | bytes 5013508
